TPU v7x, 128 devices: a whole 4x4x4 slice. The times are simulated.
128 devices in a mesh: section: 8 (over y_lo, z), replica: 16 (over x, y_hi, core).
Axes of the slice: x: 4, y: 4 (y_hi: 2, y_lo: 2; y = y_hi * 2 + y_lo), z: 4, core: 2. Of those that a mesh axis runs over, the one named last changes fastest.
Arguments:
- arriving: bfloat16 [8, 16, 6, 64, 2560], P('section', 'replica'), may hold values from -6 to 6
- stash: bfloat16 [8, 16, 6, 64, 2560], P('section', 'replica'), may hold values from -6 to 6
- cotangent: bfloat16 [8, 16, 6, 64, 2560], P('section', 'replica'), may hold values from -6 to 6
- weight: bfloat16 [8, 16, 2560, 2560], P('section', 'replica'), may hold values from -0.125 to 0.125
- gain: bfloat16 [8, 16, 2560], P('section', 'replica'), may hold values from 0.099609375 to 1.8984375
- routes_fwd: int32 [8, 96, 2], P('section'), may hold values from -1 to 15, as said below
- routes_bwd: int32 [8, 96, 2], P('section'), may hold values from -1 to 15, as said below
- partner: int32 [8, 16], P('section'), may hold values from 0 to 15, as said below
- shard_pick: int32 [8], P('section'), may hold values from 0 to 19
Outputs:
- forward_out: bfloat16 [8, 16, 6, 64, 2560], P('section', 'replica')
- backward_out: bfloat16 [8, 16, 6, 64, 2560], P('section', 'replica')
- averaged: bfloat16 [8, 16, 128, 2560], P('section', 'replica')
Inputs may be any that keep to these rules, and one draw needn't show every extreme that they name: `routes_fwd`: in each section group the live entries (both columns >= 0; -1 in both columns marks an unused entry) put at most 6 on one replica of the group and at most 6 on one replica of the neighbouring group, and no pair of replicas is named by two live entries; in every section group some replica holds exactly 6 and some receiving replica gets exactly 6. `routes_bwd`: as for routes_fwd, with the previous section group as neighbour. partner[s, partner[s, r]] = r and partner[s, r] != r.
All inputs are finite; a program needn't handle non-finite values.
Results may differ from a plain program's by a relative error of at most 0.006.
Values may be sent and summed in bfloat16 or wider, within the bound.
A program may use at most 128 MiB of HBM per device.

v0:
```python
import functools

import jax
import jax.numpy as jnp
from jax import lax
from jax.experimental import pallas as pl
from jax.experimental.pallas import tpu as pltpu
from jax.sharding import PartitionSpec as P

EPS = 1e-05
LEARN = 0.002
SLOTS = 6
TOKENS = 64
WIDTH = 2560
ROWS = SLOTS * TOKENS
SHARD = 128
XS = 4
QUARTER = WIDTH // XS
CHUNKS = 4
PART = TOKENS // CHUNKS
HELD = XS * SLOTS
TILE = 512
TILES = WIDTH // TILE
MESH = pl.DeviceIdType.MESH
BF = jnp.bfloat16
F32 = jnp.float32


def ranks(column):
    order = jnp.arange(column.shape[-1], dtype=jnp.int32)
    same = column[:, :, None] == column[:, None, :]
    before = order[None, None, :] < order[None, :, None]
    return jnp.sum((same & before).astype(jnp.int32), axis=2)


def tables(routes_fwd, routes_bwd, mates, replica):
    h = (replica // 2) % 2
    c = replica % 2
    pairs = jnp.stack([routes_fwd, routes_bwd])
    current, following = pairs[:, :, 0], pairs[:, :, 1]
    place = jnp.where(following >= 0, following * SLOTS + ranks(following), -1)
    held = jnp.where(current % 2 == c, 0, HELD) + (current // 4) * SLOTS + ranks(current)
    near = (current // 2) % 2 == h
    slot = jnp.arange(HELD, dtype=jnp.int32)
    x, t = slot // SLOTS, slot % SLOTS
    stay = ((x * 2 + h) * 2 + c) * SLOTS + t
    leave = ((x * 2 + 1 - h) * 2 + c) * SLOTS + t
    hit_stay = place[:, None, :] == stay[None, :, None]
    hit_leave = place[:, None, :] == leave[None, :, None]
    here = near[:, None, :]
    empty = 2 * HELD
    value = held[:, None, :] - empty
    keep = empty + jnp.sum(jnp.where(hit_stay & here, value, 0), axis=2)
    cross = empty + jnp.sum(jnp.where(hit_leave & here, value, 0), axis=2)
    come = jnp.any(hit_stay & ~here, axis=2)
    keep = jnp.where(come, empty + 1 + slot, keep)
    count = jnp.sum((routes_bwd[:, 0] == replica).astype(jnp.int32))
    column = jnp.arange(XS, dtype=jnp.int32)
    mine = mates[(column * 2 + h) * 2 + c]
    theirs = mates[(column * 2 + 1 - h) * 2 + c]

    def where_held(mate):
        return jnp.where(mate % 2 == c, 0, XS) + mate // 4

    mate_keep = jnp.where((mine // 2) % 2 == h, where_held(mine), 2 * XS + column)
    mate_cross = jnp.where((theirs // 2) % 2 == h, where_held(theirs), 0)
    live = (jnp.arange(SLOTS, dtype=jnp.int32) < count).astype(jnp.float32)
    return (
        jnp.concatenate(
            [cross.reshape(-1), keep.reshape(-1), mate_cross, mate_keep]
        ),
        live,
    )


CROSS, KEEP = 0, 2 * HELD
MATE_CROSS = 4 * HELD
MATE_KEEP = MATE_CROSS + XS


def kernel(table, live, gain, st_cols, gain_cols, w_rows, arr_hbm, st_hbm, ct_hbm, w_hbm, fo, bo, ao, *scratch):
    scratch = list(scratch)

    def take(n):
        out = scratch[:n]
        del scratch[:n]
        return out

    (xf, xb, yb, w, normed, dpre, dnorm, scale, upd, mu, hru, hsu, avu) = take(13)
    items = 2 * CHUNKS
    m, hr, hs, xs = take(items), take(items), take(items), take(items)
    (wsem, insem, x1s, x1r, lsem, cs, cr, hss, hsr, x2s, x2r) = take(11)

    section = lax.axis_index("section")
    replica = lax.axis_index("replica")
    x = replica // 4
    hc = replica % 4
    h, c = hc // 2, hc % 2

    def wcopy(j):
        cols = pl.ds(j * TILE, TILE)
        return pltpu.make_async_copy(w_hbm.at[:, cols], w.at[:, cols], wsem.at[j])

    loads = [
        pltpu.make_async_copy(src, dst, insem.at[i])
        for i, (src, dst) in enumerate(((arr_hbm, xf), (st_hbm, xb), (ct_hbm, yb)))
    ]
    loads[0].start()
    for j in range(TILES):
        wcopy(j).start()
    loads[1].start()
    loads[2].start()

    def at(ds, xx, hh, cc):
        return (lax.rem(section + ds + 8, 8), xx * 4 + hh * 2 + cc)

    xpeers = {d: lax.rem(x + d, XS) for d in (1, 3, 2)}
    hpeer = at(0, x, 1 - h, c)
    cpeer = at(0, x, h, 1 - c)

    barrier = pltpu.get_barrier_semaphore()
    greet = [at(0, xx, h, c) for xx in xpeers.values()] + [hpeer, cpeer]
    for ds in (1, -1):
        greet += [at(ds, xx, h, c) for xx in range(XS)]
    for device in greet:
        pl.semaphore_signal(barrier, inc=1, device_id=device, device_id_type=MESH)

    for i in range(items):
        m[i][2 * HELD] = jnp.zeros((PART, QUARTER), BF)

    def norm(src):
        g = gain[...].astype(F32)

        def block(i, _):
            v = src[i].astype(F32)
            inv = lax.rsqrt(jnp.mean(v * v, axis=-1, keepdims=True) + EPS)
            rows = pl.ds(pl.multiple_of(i * TOKENS, TOKENS), TOKENS)
            normed[rows, :] = (v * inv * g).astype(BF)
            scale[rows, :] = jnp.broadcast_to(inv, (TOKENS, 128))
            return 0

        lax.fori_loop(0, SLOTS, block, 0)

    loads[0].wait()
    norm(xf)
    for j in range(TILES):
        wcopy(j).wait()
        cols = pl.ds(j * TILE, TILE)
        pre = jnp.dot(normed[...], w[:, cols], preferred_element_type=F32)
        v = xf[:, :, cols].reshape(ROWS, TILE).astype(F32)
        out = v + pre / (1.0 + jnp.exp(-pre))
        xf[:, :, cols] = out.astype(BF).reshape(SLOTS, TOKENS, TILE)

    pl.semaphore_wait(barrier, len(greet))

    def remote(src, dst, ssem, rsem, device):
        return pltpu.make_async_remote_copy(
            src_ref=src, dst_ref=dst, send_sem=ssem, recv_sem=rsem, device_id=device, device_id_type=MESH
        )

    sends = []

    def quarter(xx):
        return pl.ds(pl.multiple_of(xx * QUARTER, 128), QUARTER)

    def spread_copies(i):
        src = xf if i < CHUNKS else yb
        rows = pl.ds((i % CHUNKS) * PART, PART)
        out = []
        for n, (d, xx) in enumerate(xpeers.items()):
            out.append(
                remote(
                    src.at[:, rows, quarter(xx)],
                    m[i].at[pl.ds(x * SLOTS, SLOTS)],
                    x1s.at[i, n],
                    x1r.at[i, n],
                    at(0, xx, h, c),
                )
            )
        own = pltpu.make_async_copy(src.at[:, rows, quarter(x)], m[i].at[pl.ds(x * SLOTS, SLOTS)], lsem.at[i])
        return out, own

    def spread(i):
        out, own = spread_copies(i)
        for cp in out:
            cp.start()
            sends.append(cp)
        own.start()

    def mirror_copy(i):
        return remote(m[i].at[pl.ds(0, HELD)], m[i].at[pl.ds(HELD, HELD)], cs.at[i], cr.at[i], cpeer)

    def mirror(i):
        out, own = spread_copies(i)
        for cp in out:
            cp.wait_recv()
        own.wait()
        cp = mirror_copy(i)
        cp.start()
        sends.append(cp)

    def cross_copy(i):
        return remote(hs[i], hr[i], hss.at[i], hsr.at[i], hpeer)

    def cross(i):
        mirror_copy(i).wait_recv()
        base = CROSS + (i // CHUNKS) * HELD

        def one(j, _):
            hs[i][j] = m[i][table[base + j]]
            return 0

        lax.fori_loop(0, HELD, one, 0)
        cp = cross_copy(i)
        cp.start()
        sends.append(cp)

    def deliver_copies(i):
        out = []
        rows = pl.ds((i % CHUNKS) * PART, PART)
        target = fo if i < CHUNKS else bo
        for d in (1, 3, 2, 0):
            xx = lax.rem(x + d, XS)
            out.append(
                remote(
                    xs[i].at[pl.ds(xx * SLOTS, SLOTS)],
                    target.at[:, rows, quarter(x)],
                    x2s.at[i, d],
                    x2r.at[i, d],
                    at(1 if i < CHUNKS else -1, xx, h, c),
                )
            )
        return out

    def deliver(i):
        cross_copy(i).wait_recv()
        base = (i // CHUNKS) * HELD

        def one(j, _):
            xs[i][j] = m[i][table[KEEP + base + j]]
            return 0

        def bring(j, _):
            m[i][2 * HELD + 1 + j] = hr[i][j]
            return 0

        lax.fori_loop(0, HELD, bring, 0)
        lax.fori_loop(0, HELD, one, 0)
        for cp in deliver_copies(i):
            cp.start()
            sends.append(cp)

    u = items

    def spread_u_copies():
        out = []
        for n, (d, xx) in enumerate(xpeers.items()):
            out.append(remote(upd.at[:, quarter(xx)], mu.at[x], x1s.at[u, n], x1r.at[u, n], at(0, xx, h, c)))
        return out, pltpu.make_async_copy(upd.at[:, quarter(x)], mu.at[x], lsem.at[u])

    def spread_u():
        out, own = spread_u_copies()
        for cp in out:
            cp.start()
            sends.append(cp)
        own.start()

    def mirror_u_copy():
        return remote(mu.at[pl.ds(0, XS)], mu.at[pl.ds(XS, XS)], cs.at[u], cr.at[u], cpeer)

    def mirror_u():
        out, own = spread_u_copies()
        for cp in out:
            cp.wait_recv()
        own.wait()
        cp = mirror_u_copy()
        cp.start()
        sends.append(cp)

    def cross_u_copy():
        return remote(hsu, hru, hss.at[u], hsr.at[u], hpeer)

    def cross_u():
        mirror_u_copy().wait_recv()

        def one(j, _):
            hsu[j] = mu[table[MATE_CROSS + j]]
            return 0

        lax.fori_loop(0, XS, one, 0)
        cp = cross_u_copy()
        cp.start()
        sends.append(cp)

    def deliver_u_copies():
        out = []
        for n, (d, xx) in enumerate(xpeers.items()):
            out.append(remote(avu.at[xx], ao.at[:, quarter(x)], x2s.at[u, n], x2r.at[u, n], at(0, xx, h, c)))
        return out, pltpu.make_async_copy(avu.at[x], ao.at[:, quarter(x)], x2r.at[u, 3])

    def deliver_u():
        cross_u_copy().wait_recv()

        def one(j, _):
            mate = mu[table[MATE_KEEP + j]]
            avu[j] = ((mu[j].astype(F32) + mate.astype(F32)) * 0.5).astype(BF)
            return 0

        for j in range(XS):
            mu[2 * XS + j] = hru[j]
        lax.fori_loop(0, XS, one, 0)
        out, own = deliver_u_copies()
        for cp in out:
            cp.start()
            sends.append(cp)
        own.start()

    for i in range(CHUNKS):
        spread(i)

    loads[1].wait()
    loads[2].wait()
    norm(xb)
    for j in range(TILES):
        if j == 2:
            mirror(0)
        if j == 3:
            cross(0)
        if j == 4:
            mirror(1)
        cols = pl.ds(j * TILE, TILE)
        pre = jnp.dot(normed[...], w[:, cols], preferred_element_type=F32)
        sig = 1.0 / (1.0 + jnp.exp(-pre))
        v = yb[:, :, cols].reshape(ROWS, TILE).astype(F32)
        d = v * sig * (1.0 + pre * (1.0 - sig))
        for i in range(SLOTS):
            rows = slice(i * TOKENS, (i + 1) * TOKENS)
            dpre[rows, cols] = (d[rows] * live[i]).astype(BF)
    cross(1)
    picked = st_cols[...].reshape(ROWS, SHARD).astype(F32)
    columns = (picked * scale[...] * gain_cols[...].astype(F32)).astype(BF)
    for j in range(TILES):
        cols = pl.ds(j * TILE, TILE)
        grad = lax.dot_general(columns, dpre[:, cols], (((0,), (0,)), ((), ())), preferred_element_type=F32)
        upd[:, cols] = (w_rows[:, cols].astype(F32) - LEARN * grad).astype(BF)
    spread_u()
    mirror(2)
    cross(2)
    for j in range(TILES):
        if j == 2:
            mirror(3)
        if j == 3:
            cross(3)
        rows = pl.ds(j * TILE, TILE)
        dnorm[:, rows] = lax.dot_general(
            dpre[...], w[rows, :], (((1,), (1,)), ((), ())), preferred_element_type=F32
        )

    def finish(k):
        g = gain[...].astype(F32)

        def block(i, _):
            rows = pl.ds(pl.multiple_of(i * TOKENS + k * PART, PART), PART)
            part = pl.ds(k * PART, PART)
            weighted = dnorm[rows, :] * g
            v = xb[i, part, :].astype(F32)
            inv = scale[rows, 0:1]
            mean = jnp.mean(weighted * v, axis=-1, keepdims=True)
            out = yb[i, part, :].astype(F32) + inv * (weighted - v * inv * inv * mean)
            yb[i, part, :] = out.astype(BF)
            return 0

        lax.fori_loop(0, SLOTS, block, 0)

    for k in range(CHUNKS):
        finish(k)
        spread(CHUNKS + k)

    mirror_u()
    deliver(0)
    cross_u()
    order = list(range(items))
    for k in range(CHUNKS):
        mirror(CHUNKS + k)
        if k + 1 < CHUNKS:
            deliver(k + 1)
        cross(CHUNKS + k)
    deliver_u()
    for k in range(CHUNKS):
        deliver(CHUNKS + k)

    for i in range(items):
        for cp in deliver_copies(i):
            cp.wait_recv()
    out, own = deliver_u_copies()
    for cp in out:
        cp.wait_recv()
    own.wait()
    for cp in sends:
        cp.wait_send()


def body(arriving, stash, cotangent, weight, gain, routes_fwd, routes_bwd, partner, shard_pick):
    replica = lax.axis_index("replica")
    table, live = tables(routes_fwd[0], routes_bwd[0], partner[0], replica)
    items = 2 * CHUNKS
    dma = pltpu.SemaphoreType.DMA
    block = (HELD, PART, QUARTER)
    whole = (SLOTS, TOKENS, WIDTH)
    scratch = [
        pltpu.VMEM(whole, BF),
        pltpu.VMEM(whole, BF),
        pltpu.VMEM(whole, BF),
        pltpu.VMEM((WIDTH, WIDTH), BF),
        pltpu.VMEM((ROWS, WIDTH), BF),
        pltpu.VMEM((ROWS, WIDTH), BF),
        pltpu.VMEM((ROWS, WIDTH), F32),
        pltpu.VMEM((ROWS, 128), F32),
        pltpu.VMEM((SHARD, WIDTH), BF),
        pltpu.VMEM((3 * XS, SHARD, QUARTER), BF),
        pltpu.VMEM((XS, SHARD, QUARTER), BF),
        pltpu.VMEM((XS, SHARD, QUARTER), BF),
        pltpu.VMEM((XS, SHARD, QUARTER), BF),
    ]
    scratch += [pltpu.VMEM((3 * HELD + 1, PART, QUARTER), BF)] * items
    scratch += [pltpu.VMEM(block, BF)] * (3 * items)
    scratch += [
        dma((TILES,)),
        dma((3,)),
        dma((items + 1, 3)),
        dma((items + 1, 3)),
        dma((items + 1,)),
        dma((items + 1,)),
        dma((items + 1,)),
        dma((items + 1,)),
        dma((items + 1,)),
        dma((items + 1, 4)),
        dma((items + 1, 4)),
    ]
    start = shard_pick[0] * SHARD
    st_cols = lax.dynamic_slice_in_dim(stash[0, 0], start, SHARD, 2)
    gain_cols = lax.dynamic_slice_in_dim(gain[0], start, SHARD, 1)
    w_rows = lax.dynamic_slice_in_dim(weight[0, 0], start, SHARD, 0)
    anywhere = pl.BlockSpec(memory_space=pl.ANY)
    forward_out, backward_out, averaged = pl.pallas_call(
        kernel,
        out_shape=[
            jax.ShapeDtypeStruct(whole, BF),
            jax.ShapeDtypeStruct(whole, BF),
            jax.ShapeDtypeStruct((SHARD, WIDTH), BF),
        ],
        in_specs=[
            pl.BlockSpec(memory_space=pltpu.SMEM),
            pl.BlockSpec(memory_space=pltpu.SMEM),
            pl.BlockSpec(memory_space=pltpu.VMEM),
            pl.BlockSpec(memory_space=pltpu.VMEM),
            pl.BlockSpec(memory_space=pltpu.VMEM),
            pl.BlockSpec(memory_space=pltpu.VMEM),
            anywhere,
            anywhere,
            anywhere,
            anywhere,
        ],
        out_specs=[anywhere] * 3,
        scratch_shapes=scratch,
        compiler_params=pltpu.CompilerParams(
            collective_id=0, has_side_effects=True, vmem_limit_bytes=63 * 2**20
        ),
        name="replica_step",
    )(table, live, gain[0], st_cols, gain_cols, w_rows, arriving[0, 0], stash[0, 0], cotangent[0, 0], weight[0, 0])
    return forward_out[None, None], backward_out[None, None], averaged[None, None]


def solution(mesh):
    in_specs = (
        P("section", "replica", None, None, None),
        P("section", "replica", None, None, None),
        P("section", "replica", None, None, None),
        P("section", "replica", None, None),
        P("section", "replica", None),
        P("section", None, None),
        P("section", None, None),
        P("section", None),
        P("section"),
    )
    out_specs = (
        P("section", "replica", None, None, None),
        P("section", "replica", None, None, None),
        P("section", "replica", None, None),
    )
    return jax.shard_map(body, mesh=mesh, in_specs=in_specs, out_specs=out_specs, check_vma=False)
```

profile of v0, /device:TPU:65, one launch (start us, length us, event | category | flops | bytes accessed | tf_op | source)
XLA Modules:
  0.0 201.9 jit_solution(5547540846136476016)
XLA Ops:
  0.6 0.0 copy-start
  1.3 1.3 fusion.12
  2.6 1.2 compare_convert_fusion.live
  3.8 0.0 copy-done
  3.8 1.2 fusion.8.gain_cols
  5.1 0.7 fusion.3
  5.8 0.7 fusion.17
  6.5 0.6 gather_fusion.1
  7.1 0.6 gather_fusion
  7.8 0.2 convert_reduce_fusion
  8.1 0.2 fusion
  8.3 0.2 select_reduce_fusion.1
  8.5 0.1 add.270
  8.6 0.1 select_n.200
  8.7 0.6 pad_add_fusion.1.table
  9.3 1.5 dynamic-slice_bitcast_fusion.1.st_cols
  10.8 2.0 dynamic-slice_bitcast_fusion.w_rows
  12.8 183.7 %replica_step.1 = (bf16[6,64,2560]{2,1,0:T(8,128)(2,1)}, bf16[6,64,2560]{2,1,0:T(8,128)(2,1)}, bf16[128,2560]{1,0:T(8,128)(2,1)}) custom-call(s32[104]{0:T(128)} %pad_add_fusion.1.table, f32[6]{0:T(128)} %compare_convert_fusion.live, bf16[1,2560]{1,0:T(2,128)(2,1)} %bitcast.37, bf16[6,64,128]{2,1,0:T(8,128)(2,1)} %dynamic-slice_bitcast_fusion.1.st_cols, ...), custom_call_target="tpu_custom_call" | custom-call | tf_op jit(solution)/shard_map/replica_step/pallas_call | solution.py:445
  196.4 0.0 copy-start.1
  196.4 3.1 %copy.20 = bf16[1,1,6,64,2560]{4,3,2,1,0:T(8,128)(2,1)} copy(bf16[1,1,6,64,2560]{4,3,2,1,0:T(8,128)(2,1)} %bitcast.35) | data formatting | bytes 3932160
  199.6 0.0 copy-done.1
  199.6 0.0 copy-start.2
  199.6 1.3 copy.21
  200.8 0.3 copy-done.2
  201.1 0.8 copy.22
  (11 shorter events, 0.1 us)
Async XLA Ops:
  0.6 3.2 %copy-start = (s32[1,16]{1,0:T(1,128)S(1)}, s32[1,16]{1,0:T(1,128)}, u32[]{:S(2)}) copy-start(s32[1,16]{1,0:T(1,128)} %param.16) | copy-start | bytes 196
  196.4 3.1 %copy-start.1 = (bf16[6,64,2560]{2,1,0:T(8,128)(2,1)S(1)}, bf16[6,64,2560]{2,1,0:T(8,128)(2,1)}, u32[]{:S(2)}) copy-start(bf16[6,64,2560]{2,1,0:T(8,128)(2,1)} %get-tuple-element.7) | copy-start | bytes 5898244
  199.6 1.5 copy-start.2
where the time goes:
time: 202 us
  Pallas kernels  184 us (91%)
  local copies, waits for them, and re-layouts  11.7 us (6%)
  other arithmetic  5.2 us (3%)
    pallas_call x1, Pallas kernels, body(): pl.pallas_call(kernel, out_shape=[jax.ShapeDtypeStruct(whole, BF), jax.Sh...  184 us
    unnamed x9, local copies, waits for them, and re-layouts  5.51 us

commit v1 on v0

--- a/solution.py
+++ b/solution.py
@@ -26,59 +26,65 @@
 F32 = jnp.float32
 
 
+def as_row(column):
+    n = column.shape[0]
+    eye = lax.broadcasted_iota(jnp.int32, (n, n), 0) == lax.broadcasted_iota(jnp.int32, (n, n), 1)
+    return jnp.sum(jnp.where(eye, column, 0), axis=0, keepdims=True)
+
+
+def as_column(row):
+    n = row.shape[1]
+    eye = lax.broadcasted_iota(jnp.int32, (n, n), 0) == lax.broadcasted_iota(jnp.int32, (n, n), 1)
+    return jnp.sum(jnp.where(eye, row, 0), axis=1, keepdims=True)
+
+
 def ranks(column):
-    order = jnp.arange(column.shape[-1], dtype=jnp.int32)
-    same = column[:, :, None] == column[:, None, :]
-    before = order[None, None, :] < order[None, :, None]
-    return jnp.sum((same & before).astype(jnp.int32), axis=2)
-
-
-def tables(routes_fwd, routes_bwd, mates, replica):
-    h = (replica // 2) % 2
-    c = replica % 2
-    pairs = jnp.stack([routes_fwd, routes_bwd])
-    current, following = pairs[:, :, 0], pairs[:, :, 1]
+    n = column.shape[0]
+    earlier = lax.broadcasted_iota(jnp.int32, (n, n), 1) < lax.broadcasted_iota(jnp.int32, (n, n), 0)
+    same = (as_row(column) == column) & earlier
+    return jnp.sum(jnp.where(same, 1, 0), axis=1, keepdims=True)
+
+
+def route_rows(pairs, h, c):
+    current, following = as_column(pairs[0:1, :]), as_column(pairs[1:2, :])
     place = jnp.where(following >= 0, following * SLOTS + ranks(following), -1)
-    held = jnp.where(current % 2 == c, 0, HELD) + (current // 4) * SLOTS + ranks(current)
-    near = (current // 2) % 2 == h
-    slot = jnp.arange(HELD, dtype=jnp.int32)
-    x, t = slot // SLOTS, slot % SLOTS
-    stay = ((x * 2 + h) * 2 + c) * SLOTS + t
-    leave = ((x * 2 + 1 - h) * 2 + c) * SLOTS + t
-    hit_stay = place[:, None, :] == stay[None, :, None]
-    hit_leave = place[:, None, :] == leave[None, :, None]
-    here = near[:, None, :]
-    empty = 2 * HELD
-    value = held[:, None, :] - empty
-    keep = empty + jnp.sum(jnp.where(hit_stay & here, value, 0), axis=2)
-    cross = empty + jnp.sum(jnp.where(hit_leave & here, value, 0), axis=2)
-    come = jnp.any(hit_stay & ~here, axis=2)
-    keep = jnp.where(come, empty + 1 + slot, keep)
-    count = jnp.sum((routes_bwd[:, 0] == replica).astype(jnp.int32))
-    column = jnp.arange(XS, dtype=jnp.int32)
-    mine = mates[(column * 2 + h) * 2 + c]
-    theirs = mates[(column * 2 + 1 - h) * 2 + c]
-
-    def where_held(mate):
-        return jnp.where(mate % 2 == c, 0, XS) + mate // 4
-
-    mate_keep = jnp.where((mine // 2) % 2 == h, where_held(mine), 2 * XS + column)
-    mate_cross = jnp.where((theirs // 2) % 2 == h, where_held(theirs), 0)
-    live = (jnp.arange(SLOTS, dtype=jnp.int32) < count).astype(jnp.float32)
-    return (
-        jnp.concatenate(
-            [cross.reshape(-1), keep.reshape(-1), mate_cross, mate_keep]
-        ),
-        live,
-    )
-
-
-CROSS, KEEP = 0, 2 * HELD
-MATE_CROSS = 4 * HELD
-MATE_KEEP = MATE_CROSS + XS
-
-
-def kernel(table, live, gain, st_cols, gain_cols, w_rows, arr_hbm, st_hbm, ct_hbm, w_hbm, fo, bo, ao, *scratch):
+    held = jnp.where((current & 1) == c, 0, HELD) + (current >> 2) * SLOTS + ranks(current)
+    near = ((current >> 1) & 1) == h
+    value = jnp.where(near, held - 2 * HELD, 0)
+    slot = lax.broadcasted_iota(jnp.int32, (1, 128), 1)
+    column = jnp.zeros_like(slot)
+    for k in range(1, XS):
+        column = column + jnp.where(slot >= k * SLOTS, 1, 0)
+    t = slot - column * SLOTS
+
+    def look(hh):
+        wanted = jnp.where(slot < HELD, ((column * 2 + hh) * 2 + c) * SLOTS + t, -2)
+        index = 2 * HELD + jnp.sum(jnp.where(place == wanted, value, 0), axis=0, keepdims=True)
+        return jnp.minimum(jnp.maximum(index, 0), 2 * HELD)
+
+    return look(1 - h), look(h)
+
+
+def mate_rows(mates, h, c):
+    slot = lax.broadcasted_iota(jnp.int32, (1, 128), 1)
+    number = lax.broadcasted_iota(jnp.int32, (mates.shape[1], 1), 0)
+    column = as_column(mates)
+
+    def mate_of(hh):
+        return jnp.sum(jnp.where(number == (slot * 2 + hh) * 2 + c, column, 0), axis=0, keepdims=True)
+
+    def found(mate, otherwise):
+        here = jnp.where((mate & 1) == c, 0, XS) + (mate >> 2)
+        return jnp.where(((mate >> 1) & 1) == h, here, otherwise)
+
+    return found(mate_of(1 - h), 0), found(mate_of(h), 2 * XS + (slot & 3))
+
+
+CROSS, KEEP = (0, 2), (1, 3)
+MATE_CROSS, MATE_KEEP = 4, 5
+
+
+def kernel(pick, gain, routes_fwd, routes_bwd, partner, arr_hbm, st_hbm, ct_hbm, w_hbm, fo, bo, ao, *scratch):
     scratch = list(scratch)
 
     def take(n):
@@ -86,20 +92,23 @@
         del scratch[:n]
         return out
 
-    (xf, xb, yb, w, normed, dpre, dnorm, scale, upd, mu, hru, hsu, avu) = take(13)
+    (xf, xb, yb, w, normed, dpre, dnorm, scale, upd, mu, hru, hsu, avu, rows_v, table, live) = take(16)
     items = 2 * CHUNKS
-    m, hr, hs, xs = take(items), take(items), take(items), take(items)
-    (wsem, insem, x1s, x1r, lsem, cs, cr, hss, hsr, x2s, x2r) = take(11)
+    m, hr, hs, ht, hts = take(items), take(items), take(items), take(items), take(items)
+    xs = hs
+    (wsem, insem, x1s, x1r, lsem, cs, cr, hss, hsr, hts_s, hts_r, x2s, x2r) = take(13)
 
     section = lax.axis_index("section")
     replica = lax.axis_index("replica")
     x = replica // 4
     hc = replica % 4
     h, c = hc // 2, hc % 2
+    y, z = section // 4, section % 4
+    turns = (z == 3, z == 0)
 
     def wcopy(j):
         cols = pl.ds(j * TILE, TILE)
-        return pltpu.make_async_copy(w_hbm.at[:, cols], w.at[:, cols], wsem.at[j])
+        return pltpu.make_async_copy(w_hbm.at[:, :, cols], w.at[:, :, cols], wsem.at[j])
 
     loads = [
         pltpu.make_async_copy(src, dst, insem.at[i])
@@ -111,17 +120,25 @@
     loads[1].start()
     loads[2].start()
 
-    def at(ds, xx, hh, cc):
-        return (lax.rem(section + ds + 8, 8), xx * 4 + hh * 2 + cc)
+    def at(xx, hh, cc):
+        return (section, xx * 4 + hh * 2 + cc)
+
+    def next_z(k, xx):
+        return (y * 4 + lax.rem(z + (1, 3)[k], 4), xx * 4 + h * 2 + c)
+
+    def across(k, hh):
+        yy = jnp.where(turns[k], 1 - y, y)
+        return (yy * 4 + z, x * 4 + hh * 2 + c)
 
     xpeers = {d: lax.rem(x + d, XS) for d in (1, 3, 2)}
-    hpeer = at(0, x, 1 - h, c)
-    cpeer = at(0, x, h, 1 - c)
+    hpeer = at(x, 1 - h, c)
+    cpeer = at(x, h, 1 - c)
 
     barrier = pltpu.get_barrier_semaphore()
-    greet = [at(0, xx, h, c) for xx in xpeers.values()] + [hpeer, cpeer]
-    for ds in (1, -1):
-        greet += [at(ds, xx, h, c) for xx in range(XS)]
+    greet = [at(xx, h, c) for xx in xpeers.values()] + [hpeer, cpeer]
+    for k in (0, 1):
+        greet += [next_z(k, xx) for xx in range(XS)]
+    greet += [((1 - y) * 4 + z, x * 4 + hh * 2 + c) for hh in (0, 1)]
     for device in greet:
         pl.semaphore_signal(barrier, inc=1, device_id=device, device_id_type=MESH)
 
@@ -141,12 +158,25 @@
 
         lax.fori_loop(0, SLOTS, block, 0)
 
+    for k, pairs in enumerate((routes_fwd[...], routes_bwd[...])):
+        leave, stay = route_rows(pairs, h, c)
+        rows_v[CROSS[k] : CROSS[k] + 1, :] = leave
+        rows_v[KEEP[k] : KEEP[k] + 1, :] = stay
+    leave, stay = mate_rows(partner[...], h, c)
+    rows_v[MATE_CROSS : MATE_CROSS + 1, :] = leave
+    rows_v[MATE_KEEP : MATE_KEEP + 1, :] = stay
+    rows_v[6:8, :] = jnp.zeros((2, 128), jnp.int32)
+    to_scalars = pltpu.make_async_copy(rows_v, table, insem.at[3])
+    to_scalars.start()
+    count = jnp.sum(jnp.where(routes_bwd[0:1, :] == replica, 1, 0), axis=1, keepdims=True)
+    live[...] = jnp.where(lax.broadcasted_iota(jnp.int32, (8, 128), 0) < count, 1.0, 0.0)
+
     loads[0].wait()
     norm(xf)
     for j in range(TILES):
         wcopy(j).wait()
         cols = pl.ds(j * TILE, TILE)
-        pre = jnp.dot(normed[...], w[:, cols], preferred_element_type=F32)
+        pre = jnp.dot(normed[...], w[:, :, cols].reshape(WIDTH, TILE), preferred_element_type=F32)
         v = xf[:, :, cols].reshape(ROWS, TILE).astype(F32)
         out = v + pre / (1.0 + jnp.exp(-pre))
         xf[:, :, cols] = out.astype(BF).reshape(SLOTS, TOKENS, TILE)
@@ -174,7 +204,7 @@
                     m[i].at[pl.ds(x * SLOTS, SLOTS)],
                     x1s.at[i, n],
                     x1r.at[i, n],
-                    at(0, xx, h, c),
+                    at(xx, h, c),
                 )
             )
         own = pltpu.make_async_copy(src.at[:, rows, quarter(x)], m[i].at[pl.ds(x * SLOTS, SLOTS)], lsem.at[i])
@@ -200,20 +230,35 @@
         sends.append(cp)
 
     def cross_copy(i):
-        return remote(hs[i], hr[i], hss.at[i], hsr.at[i], hpeer)
+        return remote(hs[i], hr[i], hss.at[i], hsr.at[i], across(i // CHUNKS, 1 - h))
+
+    def turn_copy(i):
+        return remote(hts[i], ht[i], hts_s.at[i], hts_r.at[i], across(i // CHUNKS, h))
 
     def cross(i):
         mirror_copy(i).wait_recv()
-        base = CROSS + (i // CHUNKS) * HELD
-
-        def one(j, _):
-            hs[i][j] = m[i][table[base + j]]
-            return 0
-
-        lax.fori_loop(0, HELD, one, 0)
-        cp = cross_copy(i)
-        cp.start()
-        sends.append(cp)
+        if i == 0:
+            to_scalars.wait()
+        k = i // CHUNKS
+
+        def pack(target, row):
+            def one(j, _):
+                target[j] = m[i][table[row, j]]
+                return 0
+
+            lax.fori_loop(0, HELD, one, 0)
+
+        pack(hs[i], CROSS[k])
+        cross_copy(i).start()
+
+        @pl.when(turns[k])
+        def _():
+            pack(hts[i], KEEP[k])
+            turn_copy(i).start()
+
+        @pl.when(jnp.logical_not(turns[k]))
+        def _():
+            pack(ht[i], KEEP[k])
 
     def deliver_copies(i):
         out = []
@@ -227,24 +272,24 @@
                     target.at[:, rows, quarter(x)],
                     x2s.at[i, d],
                     x2r.at[i, d],
-                    at(1 if i < CHUNKS else -1, xx, h, c),
+                    next_z(i // CHUNKS, xx),
                 )
             )
         return out
 
     def deliver(i):
         cross_copy(i).wait_recv()
-        base = (i // CHUNKS) * HELD
+
+        @pl.when(turns[i // CHUNKS])
+        def _():
+            turn_copy(i).wait()
+
+        cross_copy(i).wait_send()
 
         def one(j, _):
-            xs[i][j] = m[i][table[KEEP + base + j]]
+            xs[i][j] = hr[i][j] + ht[i][j]
             return 0
 
-        def bring(j, _):
-            m[i][2 * HELD + 1 + j] = hr[i][j]
-            return 0
-
-        lax.fori_loop(0, HELD, bring, 0)
         lax.fori_loop(0, HELD, one, 0)
         for cp in deliver_copies(i):
             cp.start()
@@ -255,7 +300,7 @@
     def spread_u_copies():
         out = []
         for n, (d, xx) in enumerate(xpeers.items()):
-            out.append(remote(upd.at[:, quarter(xx)], mu.at[x], x1s.at[u, n], x1r.at[u, n], at(0, xx, h, c)))
+            out.append(remote(upd.at[:, quarter(xx)], mu.at[x], x1s.at[u, n], x1r.at[u, n], at(xx, h, c)))
         return out, pltpu.make_async_copy(upd.at[:, quarter(x)], mu.at[x], lsem.at[u])
 
     def spread_u():
@@ -284,7 +329,7 @@
         mirror_u_copy().wait_recv()
 
         def one(j, _):
-            hsu[j] = mu[table[MATE_CROSS + j]]
+            hsu[j] = mu[table[MATE_CROSS, j]]
             return 0
 
         lax.fori_loop(0, XS, one, 0)
@@ -295,14 +340,14 @@
     def deliver_u_copies():
         out = []
         for n, (d, xx) in enumerate(xpeers.items()):
-            out.append(remote(avu.at[xx], ao.at[:, quarter(x)], x2s.at[u, n], x2r.at[u, n], at(0, xx, h, c)))
+            out.append(remote(avu.at[xx], ao.at[:, quarter(x)], x2s.at[u, n], x2r.at[u, n], at(xx, h, c)))
         return out, pltpu.make_async_copy(avu.at[x], ao.at[:, quarter(x)], x2r.at[u, 3])
 
     def deliver_u():
         cross_u_copy().wait_recv()
 
         def one(j, _):
-            mate = mu[table[MATE_KEEP + j]]
+            mate = mu[table[MATE_KEEP, j]]
             avu[j] = ((mu[j].astype(F32) + mate.astype(F32)) * 0.5).astype(BF)
             return 0
 
@@ -329,20 +374,22 @@
         if j == 4:
             mirror(1)
         cols = pl.ds(j * TILE, TILE)
-        pre = jnp.dot(normed[...], w[:, cols], preferred_element_type=F32)
+        pre = jnp.dot(normed[...], w[:, :, cols].reshape(WIDTH, TILE), preferred_element_type=F32)
         sig = 1.0 / (1.0 + jnp.exp(-pre))
         v = yb[:, :, cols].reshape(ROWS, TILE).astype(F32)
         d = v * sig * (1.0 + pre * (1.0 - sig))
         for i in range(SLOTS):
             rows = slice(i * TOKENS, (i + 1) * TOKENS)
-            dpre[rows, cols] = (d[rows] * live[i]).astype(BF)
+            dpre[rows, cols] = (d[rows] * live[i : i + 1, 0:1]).astype(BF)
     cross(1)
-    picked = st_cols[...].reshape(ROWS, SHARD).astype(F32)
-    columns = (picked * scale[...] * gain_cols[...].astype(F32)).astype(BF)
+    feature = lax.broadcasted_iota(jnp.int32, (WIDTH, SHARD), 0)
+    wanted = lax.broadcasted_iota(jnp.int32, (WIDTH, SHARD), 1) + pick[0] * SHARD
+    select = jnp.where(feature == wanted, 1.0, 0.0).astype(BF)
+    columns = jnp.dot(normed[...], select, preferred_element_type=F32).astype(BF)
     for j in range(TILES):
         cols = pl.ds(j * TILE, TILE)
         grad = lax.dot_general(columns, dpre[:, cols], (((0,), (0,)), ((), ())), preferred_element_type=F32)
-        upd[:, cols] = (w_rows[:, cols].astype(F32) - LEARN * grad).astype(BF)
+        upd[:, cols] = (w[pick[0], :, cols].astype(F32) - LEARN * grad).astype(BF)
     spread_u()
     mirror(2)
     cross(2)
@@ -353,7 +400,7 @@
             cross(3)
         rows = pl.ds(j * TILE, TILE)
         dnorm[:, rows] = lax.dot_general(
-            dpre[...], w[rows, :], (((1,), (1,)), ((), ())), preferred_element_type=F32
+            dpre[...], w[4 * j : 4 * j + 4].reshape(TILE, WIDTH), (((1,), (1,)), ((), ())), preferred_element_type=F32
         )
 
     def finish(k):
@@ -400,9 +447,22 @@
         cp.wait_send()
 
 
+def hand_on(a, b, c, x, y, z, held, rows, into, out):
+    ways = [(a.at[i], held.at[i], x.at[i]) for i in range(SLOTS)]
+    ways += [(b.at[i], held.at[SLOTS + i], y.at[i]) for i in range(SLOTS)]
+    ways += [(c, rows, z)]
+    reads = [pltpu.make_async_copy(src, mid, into.at[i]) for i, (src, mid, _) in enumerate(ways)]
+    writes = [pltpu.make_async_copy(mid, dst, out.at[i]) for i, (_, mid, dst) in enumerate(ways)]
+    for read in reads:
+        read.start()
+    for read, write in zip(reads, writes):
+        read.wait()
+        write.start()
+    for write in writes:
+        write.wait()
+
+
 def body(arriving, stash, cotangent, weight, gain, routes_fwd, routes_bwd, partner, shard_pick):
-    replica = lax.axis_index("replica")
-    table, live = tables(routes_fwd[0], routes_bwd[0], partner[0], replica)
     items = 2 * CHUNKS
     dma = pltpu.SemaphoreType.DMA
     block = (HELD, PART, QUARTER)
@@ -411,7 +471,7 @@
         pltpu.VMEM(whole, BF),
         pltpu.VMEM(whole, BF),
         pltpu.VMEM(whole, BF),
-        pltpu.VMEM((WIDTH, WIDTH), BF),
+        pltpu.VMEM((WIDTH // SHARD, SHARD, WIDTH), BF),
         pltpu.VMEM((ROWS, WIDTH), BF),
         pltpu.VMEM((ROWS, WIDTH), BF),
         pltpu.VMEM((ROWS, WIDTH), F32),
@@ -421,14 +481,19 @@
         pltpu.VMEM((XS, SHARD, QUARTER), BF),
         pltpu.VMEM((XS, SHARD, QUARTER), BF),
         pltpu.VMEM((XS, SHARD, QUARTER), BF),
+        pltpu.VMEM((8, 128), jnp.int32),
+        pltpu.SMEM((8, 128), jnp.int32),
+        pltpu.VMEM((8, 128), F32),
     ]
-    scratch += [pltpu.VMEM((3 * HELD + 1, PART, QUARTER), BF)] * items
-    scratch += [pltpu.VMEM(block, BF)] * (3 * items)
+    scratch += [pltpu.VMEM((2 * HELD + 1, PART, QUARTER), BF)] * items
+    scratch += [pltpu.VMEM(block, BF)] * (4 * items)
     scratch += [
         dma((TILES,)),
-        dma((3,)),
+        dma((4,)),
         dma((items + 1, 3)),
         dma((items + 1, 3)),
+        dma((items + 1,)),
+        dma((items + 1,)),
         dma((items + 1,)),
         dma((items + 1,)),
         dma((items + 1,)),
@@ -437,10 +502,6 @@
         dma((items + 1, 4)),
         dma((items + 1, 4)),
     ]
-    start = shard_pick[0] * SHARD
-    st_cols = lax.dynamic_slice_in_dim(stash[0, 0], start, SHARD, 2)
-    gain_cols = lax.dynamic_slice_in_dim(gain[0], start, SHARD, 1)
-    w_rows = lax.dynamic_slice_in_dim(weight[0, 0], start, SHARD, 0)
     anywhere = pl.BlockSpec(memory_space=pl.ANY)
     forward_out, backward_out, averaged = pl.pallas_call(
         kernel,
@@ -450,7 +511,6 @@
             jax.ShapeDtypeStruct((SHARD, WIDTH), BF),
         ],
         in_specs=[
-            pl.BlockSpec(memory_space=pltpu.SMEM),
             pl.BlockSpec(memory_space=pltpu.SMEM),
             pl.BlockSpec(memory_space=pltpu.VMEM),
             pl.BlockSpec(memory_space=pltpu.VMEM),
@@ -467,7 +527,35 @@
             collective_id=0, has_side_effects=True, vmem_limit_bytes=63 * 2**20
         ),
         name="replica_step",
-    )(table, live, gain[0], st_cols, gain_cols, w_rows, arriving[0, 0], stash[0, 0], cotangent[0, 0], weight[0, 0])
+    )(
+        shard_pick,
+        gain[0],
+        jnp.swapaxes(routes_fwd[0], 0, 1),
+        jnp.swapaxes(routes_bwd[0], 0, 1),
+        partner,
+        arriving[0, 0],
+        stash[0, 0],
+        cotangent[0, 0],
+        weight.reshape(WIDTH // SHARD, SHARD, WIDTH),
+    )
+    forward_out, backward_out, averaged = pl.pallas_call(
+        hand_on,
+        out_shape=[
+            jax.ShapeDtypeStruct(whole, BF),
+            jax.ShapeDtypeStruct(whole, BF),
+            jax.ShapeDtypeStruct((SHARD, WIDTH), BF),
+        ],
+        in_specs=[anywhere] * 3,
+        out_specs=[anywhere] * 3,
+        scratch_shapes=[
+            pltpu.VMEM((2 * SLOTS, TOKENS, WIDTH), BF),
+            pltpu.VMEM((SHARD, WIDTH), BF),
+            dma((2 * SLOTS + 1,)),
+            dma((2 * SLOTS + 1,)),
+        ],
+        compiler_params=pltpu.CompilerParams(vmem_limit_bytes=63 * 2**20),
+        name="hand_on",
+    )(forward_out, backward_out, averaged)
     return forward_out[None, None], backward_out[None, None], averaged[None, None]
 
 

time: 202 us -> 151 us (0.75)
  Pallas kernels: 184 us -> 149 us
  local copies, waits for them, and re-layouts: 11.7 us -> 0 us
  other arithmetic: 5.2 us -> 0 us
    pallas_call x1, Pallas kernels: 184 us -> 144 us  [body(): pl.pallas_call(kernel, out_shape=[jax.ShapeDtypeStruct(whole, BF), jax.Sh...]
    unnamed x9 -> x0, local copies, waits for them, and re-layouts: 5.51 us -> none
    dynamic_slice x3 -> x0, local copies, waits for them, and re-layouts: 4.73 us -> none  [the longest x1 1.96 us: body(): w_rows = lax.dynamic_slice_in_dim(weight[0, 0], start, SHARD, 0)]
    pallas_call x0 -> x1, Pallas kernels: none -> 4.32 us  [body(): pl.pallas_call(hand_on, out_shape=[jax.ShapeDtypeStruct(whole, BF), jax.S...]
where the time goes in v1:
time: 151 us; the launch traced here: 150 us
  Pallas kernels  149 us (99%)
    pallas_call x1, Pallas kernels, body(): pl.pallas_call(kernel, out_shape=[jax.ShapeDtypeStruct(whole, BF), jax.Sh...  144 us
    pallas_call x1, Pallas kernels, body(): pl.pallas_call(hand_on, out_shape=[jax.ShapeDtypeStruct(whole, BF), jax.S...  4.32 us

profile of v1, /device:TPU:65, one launch (start us, length us, event | category | flops | bytes accessed | tf_op | source)
XLA Modules:
  0.0 150.2 jit_solution(2246301679373420446)
XLA Ops:
  1.3 144.4 %replica_step.1 = (bf16[6,64,2560]{2,1,0:T(8,128)(2,1)}, bf16[6,64,2560]{2,1,0:T(8,128)(2,1)}, bf16[128,2560]{1,0:T(8,128)(2,1)}) custom-call(s32[1]{0:T(128)S(6)} %copy.12.pick, bf16[1,2560]{1,0:T(2,128)(2,1)} %bitcast.18, s32[2,96]{1,0:T(2,128)} %bitcast.19, s32[2,96]{1,0:T(2,128)} %bitcast.20, s32[1,16]{1,0:T(1,128)} %partner.1, ...), custom_call_target="tpu_custom_call" | custom-call | tf_op jit(solution)/shard_map/replica_step/pallas_call | solution.py:506
  145.7 4.3 %hand_on.1 = (bf16[6,64,2560]{2,1,0:T(8,128)(2,1)}, bf16[6,64,2560]{2,1,0:T(8,128)(2,1)}, bf16[128,2560]{1,0:T(8,128)(2,1)}) custom-call(bf16[6,64,2560]{2,1,0:T(8,128)(2,1)} %get-tuple-element.9.a, bf16[6,64,2560]{2,1,0:T(8,128)(2,1)} %get-tuple-element.10.b, bf16[128,2560]{1,0:T(8,128)(2,1)} %get-tuple-element.11.c), custom_call_target="tpu_custom_call" | custom-call | tf_op jit(solution)/shard_map/hand_on/pallas_call | solution.py:541

commit v2 on v1

--- a/solution.py
+++ b/solution.py
@@ -13,6 +13,7 @@
 TOKENS = 64
 WIDTH = 2560
 ROWS = SLOTS * TOKENS
+HALF = ROWS // 2
 SHARD = 128
 XS = 4
 QUARTER = WIDTH // XS
@@ -144,6 +145,20 @@
 
     for i in range(items):
         m[i][2 * HELD] = jnp.zeros((PART, QUARTER), BF)
+
+    def norm_halves(src):
+        g = gain[...].astype(F32)
+
+        def block(i, _):
+            v = src[i].astype(F32)
+            inv = lax.rsqrt(jnp.mean(v * v, axis=-1, keepdims=True) + EPS)
+            out = (v * inv * g).astype(BF)
+            for half in range(2):
+                rows = pl.ds(pl.multiple_of(half * HALF + i * (TOKENS // 2), TOKENS // 2), TOKENS // 2)
+                normed[rows, :] = out[half * (TOKENS // 2) : (half + 1) * (TOKENS // 2)]
+            return 0
+
+        lax.fori_loop(0, SLOTS, block, 0)
 
     def norm(src):
         g = gain[...].astype(F32)
@@ -172,15 +187,24 @@
     live[...] = jnp.where(lax.broadcasted_iota(jnp.int32, (8, 128), 0) < count, 1.0, 0.0)
 
     loads[0].wait()
-    norm(xf)
-    for j in range(TILES):
-        wcopy(j).wait()
-        cols = pl.ds(j * TILE, TILE)
-        pre = jnp.dot(normed[...], w[:, :, cols].reshape(WIDTH, TILE), preferred_element_type=F32)
-        v = xf[:, :, cols].reshape(ROWS, TILE).astype(F32)
-        out = v + pre / (1.0 + jnp.exp(-pre))
-        xf[:, :, cols] = out.astype(BF).reshape(SLOTS, TOKENS, TILE)
-
+    norm_halves(xf)
+
+    def forward(half):
+        tokens = pl.ds(half * (TOKENS // 2), TOKENS // 2)
+        for j in range(TILES):
+            if half == 0:
+                wcopy(j).wait()
+            cols = pl.ds(j * TILE, TILE)
+            pre = jnp.dot(
+                normed[half * HALF : (half + 1) * HALF, :],
+                w[:, :, cols].reshape(WIDTH, TILE),
+                preferred_element_type=F32,
+            )
+            v = xf[:, tokens, cols].reshape(HALF, TILE).astype(F32)
+            out = v + pre / (1.0 + jnp.exp(-pre))
+            xf[:, tokens, cols] = out.astype(BF).reshape(SLOTS, TOKENS // 2, TILE)
+
+    forward(0)
     pl.semaphore_wait(barrier, len(greet))
 
     def remote(src, dst, ssem, rsem, device):
@@ -229,11 +253,18 @@
         cp.start()
         sends.append(cp)
 
-    def cross_copy(i):
-        return remote(hs[i], hr[i], hss.at[i], hsr.at[i], across(i // CHUNKS, 1 - h))
-
-    def turn_copy(i):
-        return remote(hts[i], ht[i], hts_s.at[i], hts_r.at[i], across(i // CHUNKS, h))
+    def part_of(p):
+        return pl.ds(p * (HELD // 2), HELD // 2)
+
+    def cross_copy(i, p):
+        return remote(
+            hs[i].at[part_of(p)], hr[i].at[part_of(p)], hss.at[i, p], hsr.at[i, p], across(i // CHUNKS, 1 - h)
+        )
+
+    def turn_copy(i, p):
+        return remote(
+            hts[i].at[part_of(p)], ht[i].at[part_of(p)], hts_s.at[i, p], hts_r.at[i, p], across(i // CHUNKS, h)
+        )
 
     def cross(i):
         mirror_copy(i).wait_recv()
@@ -241,59 +272,68 @@
             to_scalars.wait()
         k = i // CHUNKS
 
-        def pack(target, row):
+        def pack(target, row, p):
             def one(j, _):
                 target[j] = m[i][table[row, j]]
                 return 0
 
-            lax.fori_loop(0, HELD, one, 0)
-
-        pack(hs[i], CROSS[k])
-        cross_copy(i).start()
-
-        @pl.when(turns[k])
-        def _():
-            pack(hts[i], KEEP[k])
-            turn_copy(i).start()
+            lax.fori_loop(p * (HELD // 2), (p + 1) * (HELD // 2), one, 0)
+
+        for p in range(2):
+            pack(hs[i], CROSS[k], p)
+            cross_copy(i, p).start()
+
+            @pl.when(turns[k])
+            def _():
+                pack(hts[i], KEEP[k], p)
+                turn_copy(i, p).start()
 
         @pl.when(jnp.logical_not(turns[k]))
         def _():
-            pack(ht[i], KEEP[k])
-
-    def deliver_copies(i):
-        out = []
+            pack(ht[i], KEEP[k], 0)
+            pack(ht[i], KEEP[k], 1)
+
+    def deliver_copy(i, xx):
+        target = fo if i < CHUNKS else bo
         rows = pl.ds((i % CHUNKS) * PART, PART)
+        return remote(
+            xs[i].at[pl.ds(xx * SLOTS, SLOTS)],
+            target.at[:, rows, quarter(x)],
+            x2s.at[i, xx],
+            x2r.at[i, x],
+            next_z(i // CHUNKS, xx),
+        )
+
+    def delivered(i, xx):
         target = fo if i < CHUNKS else bo
-        for d in (1, 3, 2, 0):
-            xx = lax.rem(x + d, XS)
-            out.append(
-                remote(
-                    xs[i].at[pl.ds(xx * SLOTS, SLOTS)],
-                    target.at[:, rows, quarter(x)],
-                    x2s.at[i, d],
-                    x2r.at[i, d],
-                    next_z(i // CHUNKS, xx),
-                )
-            )
-        return out
+        rows = pl.ds((i % CHUNKS) * PART, PART)
+        remote(
+            xs[i].at[pl.ds(xx * SLOTS, SLOTS)],
+            target.at[:, rows, quarter(xx)],
+            x2s.at[i, xx],
+            x2r.at[i, xx],
+            next_z(i // CHUNKS, xx),
+        ).wait_recv()
 
     def deliver(i):
-        cross_copy(i).wait_recv()
-
-        @pl.when(turns[i // CHUNKS])
-        def _():
-            turn_copy(i).wait()
-
-        cross_copy(i).wait_send()
-
-        def one(j, _):
-            xs[i][j] = hr[i][j] + ht[i][j]
-            return 0
-
-        lax.fori_loop(0, HELD, one, 0)
-        for cp in deliver_copies(i):
-            cp.start()
-            sends.append(cp)
+        for p in range(2):
+            cross_copy(i, p).wait_recv()
+
+            @pl.when(turns[i // CHUNKS])
+            def _():
+                turn_copy(i, p).wait()
+
+            cross_copy(i, p).wait_send()
+
+            def one(j, _):
+                xs[i][j] = hr[i][j] + ht[i][j]
+                return 0
+
+            lax.fori_loop(p * (HELD // 2), (p + 1) * (HELD // 2), one, 0)
+            for xx in (2 * p, 2 * p + 1):
+                cp = deliver_copy(i, xx)
+                cp.start()
+                sends.append(cp)
 
     u = items
 
@@ -323,7 +363,7 @@
         sends.append(cp)
 
     def cross_u_copy():
-        return remote(hsu, hru, hss.at[u], hsr.at[u], hpeer)
+        return remote(hsu, hru, hss.at[u, 0], hsr.at[u, 0], hpeer)
 
     def cross_u():
         mirror_u_copy().wait_recv()
@@ -360,19 +400,24 @@
             sends.append(cp)
         own.start()
 
-    for i in range(CHUNKS):
-        spread(i)
+    spread(0)
+    spread(1)
+    forward(1)
+    spread(2)
+    spread(3)
 
     loads[1].wait()
     loads[2].wait()
     norm(xb)
     for j in range(TILES):
+        if j == 1:
+            mirror(0)
         if j == 2:
-            mirror(0)
+            cross(0)
         if j == 3:
-            cross(0)
+            mirror(1)
         if j == 4:
-            mirror(1)
+            cross(1)
         cols = pl.ds(j * TILE, TILE)
         pre = jnp.dot(normed[...], w[:, :, cols].reshape(WIDTH, TILE), preferred_element_type=F32)
         sig = 1.0 / (1.0 + jnp.exp(-pre))
@@ -381,7 +426,7 @@
         for i in range(SLOTS):
             rows = slice(i * TOKENS, (i + 1) * TOKENS)
             dpre[rows, cols] = (d[rows] * live[i : i + 1, 0:1]).astype(BF)
-    cross(1)
+    mirror(2)
     feature = lax.broadcasted_iota(jnp.int32, (WIDTH, SHARD), 0)
     wanted = lax.broadcasted_iota(jnp.int32, (WIDTH, SHARD), 1) + pick[0] * SHARD
     select = jnp.where(feature == wanted, 1.0, 0.0).astype(BF)
@@ -391,13 +436,12 @@
         grad = lax.dot_general(columns, dpre[:, cols], (((0,), (0,)), ((), ())), preferred_element_type=F32)
         upd[:, cols] = (w[pick[0], :, cols].astype(F32) - LEARN * grad).astype(BF)
     spread_u()
-    mirror(2)
-    cross(2)
     for j in range(TILES):
-        if j == 2:
+        if j == 1:
+            deliver(0)
+            cross(2)
+        if j == 3:
             mirror(3)
-        if j == 3:
-            cross(3)
         rows = pl.ds(j * TILE, TILE)
         dnorm[:, rows] = lax.dot_general(
             dpre[...], w[4 * j : 4 * j + 4].reshape(TILE, WIDTH), (((1,), (1,)), ((), ())), preferred_element_type=F32
@@ -423,22 +467,29 @@
         finish(k)
         spread(CHUNKS + k)
 
+    deliver(1)
+    cross(3)
     mirror_u()
-    deliver(0)
+    deliver(2)
     cross_u()
-    order = list(range(items))
-    for k in range(CHUNKS):
-        mirror(CHUNKS + k)
-        if k + 1 < CHUNKS:
-            deliver(k + 1)
-        cross(CHUNKS + k)
+    mirror(4)
+    deliver(3)
+    cross(4)
+    mirror(5)
     deliver_u()
-    for k in range(CHUNKS):
-        deliver(CHUNKS + k)
+    cross(5)
+    mirror(6)
+    deliver(4)
+    cross(6)
+    mirror(7)
+    deliver(5)
+    cross(7)
+    deliver(6)
+    deliver(7)
 
     for i in range(items):
-        for cp in deliver_copies(i):
-            cp.wait_recv()
+        for xx in range(XS):
+            delivered(i, xx)
     out, own = deliver_u_copies()
     for cp in out:
         cp.wait_recv()
@@ -495,10 +546,10 @@
         dma((items + 1,)),
         dma((items + 1,)),
         dma((items + 1,)),
-        dma((items + 1,)),
-        dma((items + 1,)),
-        dma((items + 1,)),
-        dma((items + 1,)),
+        dma((items + 1, 2)),
+        dma((items + 1, 2)),
+        dma((items + 1, 2)),
+        dma((items + 1, 2)),
         dma((items + 1, 4)),
         dma((items + 1, 4)),
     ]

time: 151 us -> 143 us (0.947)
  Pallas kernels: 149 us -> 140 us
    pallas_call x1, Pallas kernels: 144 us -> 136 us  [body(): pl.pallas_call(kernel, out_shape=[jax.ShapeDtypeStruct(whole, BF), jax.Sh...]
where the time goes in v2:
time: 143 us; the launch traced here: 142 us
  Pallas kernels  140 us (98%)
  between operations  1.45 us (1%)
    pallas_call x1, Pallas kernels, body(): pl.pallas_call(kernel, out_shape=[jax.ShapeDtypeStruct(whole, BF), jax.Sh...  136 us
    pallas_call x1, Pallas kernels, body(): pl.pallas_call(hand_on, out_shape=[jax.ShapeDtypeStruct(whole, BF), jax.S...  4.32 us

profile of v2, /device:TPU:65, one launch (start us, length us, event | category | flops | bytes accessed | tf_op | source)
XLA Modules:
  0.0 141.5 jit_solution(15366558261463753373)
XLA Ops:
  1.3 135.8 %replica_step.1 = (bf16[6,64,2560]{2,1,0:T(8,128)(2,1)}, bf16[6,64,2560]{2,1,0:T(8,128)(2,1)}, bf16[128,2560]{1,0:T(8,128)(2,1)}) custom-call(s32[1]{0:T(128)S(6)} %copy.12.pick, bf16[1,2560]{1,0:T(2,128)(2,1)} %bitcast.18, s32[2,96]{1,0:T(2,128)} %bitcast.19, s32[2,96]{1,0:T(2,128)} %bitcast.20, s32[1,16]{1,0:T(1,128)} %partner.1, ...), custom_call_target="tpu_custom_call" | custom-call | tf_op jit(solution)/shard_map/replica_step/pallas_call | solution.py:557
  137.1 4.3 %hand_on.1 = (bf16[6,64,2560]{2,1,0:T(8,128)(2,1)}, bf16[6,64,2560]{2,1,0:T(8,128)(2,1)}, bf16[128,2560]{1,0:T(8,128)(2,1)}) custom-call(bf16[6,64,2560]{2,1,0:T(8,128)(2,1)} %get-tuple-element.9.a, bf16[6,64,2560]{2,1,0:T(8,128)(2,1)} %get-tuple-element.10.b, bf16[128,2560]{1,0:T(8,128)(2,1)} %get-tuple-element.11.c), custom_call_target="tpu_custom_call" | custom-call | tf_op jit(solution)/shard_map/hand_on/pallas_call | solution.py:592

commit v3 on v2

--- a/solution.py
+++ b/solution.py
@@ -22,6 +22,7 @@
 HELD = XS * SLOTS
 TILE = 512
 TILES = WIDTH // TILE
+STEPS = (1, 3, 2, 0)
 MESH = pl.DeviceIdType.MESH
 BF = jnp.bfloat16
 F32 = jnp.float32
@@ -131,7 +132,8 @@
         yy = jnp.where(turns[k], 1 - y, y)
         return (yy * 4 + z, x * 4 + hh * 2 + c)
 
-    xpeers = {d: lax.rem(x + d, XS) for d in (1, 3, 2)}
+    places = [lax.rem(x + d, XS) for d in STEPS]
+    xpeers = dict(zip(STEPS[:3], places))
     hpeer = at(x, 1 - h, c)
     cpeer = at(x, h, 1 - c)
 
@@ -273,11 +275,13 @@
         k = i // CHUNKS
 
         def pack(target, row, p):
-            def one(j, _):
-                target[j] = m[i][table[row, j]]
-                return 0
-
-            lax.fori_loop(p * (HELD // 2), (p + 1) * (HELD // 2), one, 0)
+            for q in (2 * p, 2 * p + 1):
+
+                def one(j, _):
+                    target[q * SLOTS + j] = m[i][table[row, places[q] * SLOTS + j]]
+                    return 0
+
+                lax.fori_loop(0, SLOTS, one, 0)
 
         for p in range(2):
             pack(hs[i], CROSS[k], p)
@@ -293,27 +297,16 @@
             pack(ht[i], KEEP[k], 0)
             pack(ht[i], KEEP[k], 1)
 
-    def deliver_copy(i, xx):
+    def deliver_copy(i, q, source):
         target = fo if i < CHUNKS else bo
         rows = pl.ds((i % CHUNKS) * PART, PART)
         return remote(
-            xs[i].at[pl.ds(xx * SLOTS, SLOTS)],
-            target.at[:, rows, quarter(x)],
-            x2s.at[i, xx],
-            x2r.at[i, x],
-            next_z(i // CHUNKS, xx),
+            xs[i].at[pl.ds(q * SLOTS, SLOTS)],
+            target.at[:, rows, quarter(source)],
+            x2s.at[i, q],
+            x2r.at[i, q],
+            next_z(i // CHUNKS, places[q]),
         )
-
-    def delivered(i, xx):
-        target = fo if i < CHUNKS else bo
-        rows = pl.ds((i % CHUNKS) * PART, PART)
-        remote(
-            xs[i].at[pl.ds(xx * SLOTS, SLOTS)],
-            target.at[:, rows, quarter(xx)],
-            x2s.at[i, xx],
-            x2r.at[i, xx],
-            next_z(i // CHUNKS, xx),
-        ).wait_recv()
 
     def deliver(i):
         for p in range(2):
@@ -330,8 +323,8 @@
                 return 0
 
             lax.fori_loop(p * (HELD // 2), (p + 1) * (HELD // 2), one, 0)
-            for xx in (2 * p, 2 * p + 1):
-                cp = deliver_copy(i, xx)
+            for q in (2 * p, 2 * p + 1):
+                cp = deliver_copy(i, q, x)
                 cp.start()
                 sends.append(cp)
 
@@ -469,17 +462,17 @@
 
     deliver(1)
     cross(3)
+    mirror(4)
+    deliver(2)
+    cross(4)
     mirror_u()
-    deliver(2)
+    mirror(5)
+    deliver(3)
     cross_u()
-    mirror(4)
-    deliver(3)
-    cross(4)
-    mirror(5)
-    deliver_u()
+    deliver(4)
     cross(5)
     mirror(6)
-    deliver(4)
+    deliver_u()
     cross(6)
     mirror(7)
     deliver(5)
@@ -488,8 +481,8 @@
     deliver(7)
 
     for i in range(items):
-        for xx in range(XS):
-            delivered(i, xx)
+        for q in range(XS):
+            deliver_copy(i, q, lax.rem(x - STEPS[q] + XS, XS)).wait_recv()
     out, own = deliver_u_copies()
     for cp in out:
         cp.wait_recv()

time: 143 us -> 142 us (level)
  no operation moved by 1% of the time
where the time goes in v3:
time: 142 us; the launch traced here: 141 us
  Pallas kernels  139 us (98%)
  between operations  1.45 us (1%)
    pallas_call x1, Pallas kernels, body(): pl.pallas_call(kernel, out_shape=[jax.ShapeDtypeStruct(whole, BF), jax.Sh...  135 us
    pallas_call x1, Pallas kernels, body(): pl.pallas_call(hand_on, out_shape=[jax.ShapeDtypeStruct(whole, BF), jax.S...  4.32 us

profile of v3, /device:TPU:65, one launch (start us, length us, event | category | flops | bytes accessed | tf_op | source)
XLA Modules:
  0.0 140.9 jit_solution(18264137581791582108)
XLA Ops:
  1.3 135.1 %replica_step.1 = (bf16[6,64,2560]{2,1,0:T(8,128)(2,1)}, bf16[6,64,2560]{2,1,0:T(8,128)(2,1)}, bf16[128,2560]{1,0:T(8,128)(2,1)}) custom-call(s32[1]{0:T(128)S(6)} %copy.12.pick, bf16[1,2560]{1,0:T(2,128)(2,1)} %bitcast.18, s32[2,96]{1,0:T(2,128)} %bitcast.19, s32[2,96]{1,0:T(2,128)} %bitcast.20, s32[1,16]{1,0:T(1,128)} %partner.1, ...), custom_call_target="tpu_custom_call" | custom-call | tf_op jit(solution)/shard_map/replica_step/pallas_call | solution.py:550
  136.4 4.3 %hand_on.1 = (bf16[6,64,2560]{2,1,0:T(8,128)(2,1)}, bf16[6,64,2560]{2,1,0:T(8,128)(2,1)}, bf16[128,2560]{1,0:T(8,128)(2,1)}) custom-call(bf16[6,64,2560]{2,1,0:T(8,128)(2,1)} %get-tuple-element.9.a, bf16[6,64,2560]{2,1,0:T(8,128)(2,1)} %get-tuple-element.10.b, bf16[128,2560]{1,0:T(8,128)(2,1)} %get-tuple-element.11.c), custom_call_target="tpu_custom_call" | custom-call | tf_op jit(solution)/shard_map/hand_on/pallas_call | solution.py:585
